TPU v7x, 32 devices: a whole 2x2x4 slice. The times are simulated.
32 devices in a mesh: groups: 2 (over y), pool: 4 (over z), tensor: 4 (over x, core).
Axes of the slice: x: 2, y: 2, z: 4, core: 2. Of those that a mesh axis runs over, the one named last changes fastest.
Arguments:
- incoming_hidden: bfloat16 [4, 8, 8192], P(None, ('groups', 'pool')), parts along dimension 1, may hold values from -6 to 6
- attention_norm_gain: bfloat16 [8192], replicated, may hold values from 0.099609375 to 1.8984375
- frozen_query_weight: bfloat16 [8192, 8192], P('pool', 'tensor'), may hold values from -0.0625 to 0.0625
- frozen_key_weight: bfloat16 [8192, 1024], P('pool', 'tensor'), may hold values from -0.0625 to 0.0625
- frozen_value_weight: bfloat16 [8192, 1024], P('pool', 'tensor'), may hold values from -0.0625 to 0.0625
- frozen_output_weight: bfloat16 [8192, 8192], P('tensor', 'pool'), may hold values from -1 to 1
- query_adapter_first: bfloat16 [16384, 64], P('groups', 'pool'), parts along dimension 0, may hold values from -0.0625 to 0.0625
- query_adapter_second: bfloat16 [128, 8192], P(('groups', 'pool')), parts along dimension 0, may hold values from -0.75 to 0.75
- key_adapter_first: bfloat16 [16384, 64], P('groups', 'pool'), parts along dimension 0, may hold values from -0.0625 to 0.0625
- key_adapter_second: bfloat16 [128, 1024], P(('groups', 'pool')), parts along dimension 0, may hold values from -0.75 to 0.75
- value_adapter_first: bfloat16 [16384, 64], P('groups', 'pool'), parts along dimension 0, may hold values from -0.0625 to 0.0625
- value_adapter_second: bfloat16 [128, 1024], P(('groups', 'pool')), parts along dimension 0, may hold values from -0.75 to 0.75
- output_adapter_first: bfloat16 [16384, 64], P('groups', 'pool'), parts along dimension 0, may hold values from -1 to 1
- output_adapter_second: bfloat16 [128, 8192], P(('groups', 'pool')), parts along dimension 0, may hold values from -0.75 to 0.75
- earlier_keys: bfloat16 [8, 4096, 8, 128], P(('groups', 'pool'), None, 'tensor'), parts along dimension 0, may hold values from -1000 to 1000
- earlier_values: bfloat16 [8, 4096, 8, 128], P(('groups', 'pool'), None, 'tensor'), parts along dimension 0, may hold values from -6 to 6
- filled_lengths: int32 [8], P(('groups', 'pool')), parts along dimension 0, may hold values from 512 to 4092, as said below
Outputs:
- attn_out: bfloat16 [4, 8, 8192], P(None, 'groups', 'pool'), parts along dimension 1
There are 2 independent parts, one for each index of `groups`. A program takes and returns all parts, laid end to end along the dimension named above; an argument that names none is the same for every part. Nothing has to cross between parts.
Inputs may be any that keep to these rules, and one draw needn't show every extreme that they name: `filled_lengths`: every length lies between 512 and 4092; some row has exactly 4092 and some row exactly 512.
All inputs are finite; a program needn't handle non-finite values.
Results may differ from a plain program's by a relative error of at most 0.011.
Values may be sent and summed in bfloat16 or wider, within the bound.
A program may use at most 128 MiB of HBM per device.

v0:
```python
import jax
import jax.numpy as jnp
from jax import lax
from jax.sharding import PartitionSpec as P

rope_base = 500000.0
norm_eps = 1e-05


def rotate(values, positions):
    half_dim = values.shape[-1] // 2
    frequency = rope_base ** (-(jnp.arange(half_dim).astype(jnp.float32) * 2.0 / values.shape[-1]))
    angles = positions[..., None] * frequency
    cosine = jnp.cos(angles)
    sine = jnp.sin(angles)
    first_half = values[..., :half_dim]
    second_half = values[..., half_dim:]
    return jnp.concatenate(
        [first_half * cosine - second_half * sine, second_half * cosine + first_half * sine], -1
    )


def combine_adapter_weight(weight, factor_a, factor_b):
    return (
        weight.astype(jnp.float32) + jnp.dot(factor_a, factor_b, preferred_element_type=jnp.float32)
    ).astype(jnp.bfloat16)


def attend(queries, earlier_keys, earlier_values, new_keys, new_values, lengths, query_steps):
    decoded_row_count, steps_count, heads_count, head_dim = queries.shape
    kv_count = earlier_keys.shape[2]
    group_size = heads_count // kv_count
    scale = 1.0 / jnp.sqrt(jnp.float32(head_dim))
    grouped = queries.reshape(decoded_row_count, steps_count, kv_count, group_size, head_dim)
    scores_cache = (
        jnp.einsum("rskgd,rckd->rkgsc", grouped, earlier_keys, preferred_element_type=jnp.float32)
        * scale
    )
    scores_new = (
        jnp.einsum("rskgd,rtkd->rkgst", grouped, new_keys, preferred_element_type=jnp.float32)
        * scale
    )
    seen_cache = jnp.arange(earlier_keys.shape[1])[None, :] < lengths[:, None]
    seen_new = jnp.arange(new_keys.shape[1])[None, :] <= query_steps[:, None]
    scores_cache = jnp.where(seen_cache[:, None, None, None, :], scores_cache, -1e30)
    scores_new = jnp.where(seen_new[None, None, None, :, :], scores_new, -1e30)
    top_score = jnp.maximum(
        jnp.max(scores_cache, -1, keepdims=True), jnp.max(scores_new, -1, keepdims=True)
    )
    exp_cache = jnp.exp(scores_cache - top_score)
    exp_new = jnp.exp(scores_new - top_score)
    denominator = jnp.sum(exp_cache, -1, keepdims=True) + jnp.sum(exp_new, -1, keepdims=True)
    weights_cache = (exp_cache / denominator).astype(jnp.bfloat16)
    weights_new = (exp_new / denominator).astype(jnp.bfloat16)
    mixed = jnp.einsum(
        "rkgsc,rckd->rskgd", weights_cache, earlier_values, preferred_element_type=jnp.float32
    )
    mixed = mixed + jnp.einsum(
        "rkgst,rtkd->rskgd", weights_new, new_values, preferred_element_type=jnp.float32
    )
    return mixed.reshape(decoded_row_count, steps_count, heads_count * head_dim).astype(
        jnp.bfloat16
    )


def on_device(
    incoming_hidden,
    attention_norm_gain,
    frozen_query_weight,
    frozen_key_weight,
    frozen_value_weight,
    frozen_output_weight,
    query_adapter_first,
    query_adapter_second,
    key_adapter_first,
    key_adapter_second,
    value_adapter_first,
    value_adapter_second,
    output_adapter_first,
    output_adapter_second,
    earlier_keys,
    earlier_values,
    filled_lengths,
):
    pool_index = lax.axis_index("pool")
    tensor_index = lax.axis_index("tensor")
    feature_count = frozen_query_weight.shape[0]
    query_cols = frozen_query_weight.shape[1]
    key_cols = frozen_key_weight.shape[1]
    out_rows = frozen_output_weight.shape[0]
    down_parts = (
        lax.all_gather(query_adapter_first, "pool", axis=1, tiled=True),
        lax.all_gather(key_adapter_first, "pool", axis=1, tiled=True),
        lax.all_gather(value_adapter_first, "pool", axis=1, tiled=True),
        lax.all_gather(output_adapter_first, "pool", axis=1, tiled=True),
    )
    up_parts = (
        lax.all_gather(query_adapter_second, "pool", axis=0, tiled=True),
        lax.all_gather(key_adapter_second, "pool", axis=0, tiled=True),
        lax.all_gather(value_adapter_second, "pool", axis=0, tiled=True),
        lax.all_gather(output_adapter_second, "pool", axis=0, tiled=True),
    )
    factor_aq = lax.dynamic_slice_in_dim(
        down_parts[0], pool_index * feature_count, feature_count, 0
    )
    factor_ak = lax.dynamic_slice_in_dim(
        down_parts[1], pool_index * feature_count, feature_count, 0
    )
    factor_av = lax.dynamic_slice_in_dim(
        down_parts[2], pool_index * feature_count, feature_count, 0
    )
    factor_ao = lax.dynamic_slice_in_dim(down_parts[3], tensor_index * out_rows, out_rows, 0)
    factor_bq = lax.dynamic_slice_in_dim(up_parts[0], tensor_index * query_cols, query_cols, 1)
    factor_bk = lax.dynamic_slice_in_dim(up_parts[1], tensor_index * key_cols, key_cols, 1)
    factor_bv = lax.dynamic_slice_in_dim(up_parts[2], tensor_index * key_cols, key_cols, 1)
    factor_bo = lax.dynamic_slice_in_dim(up_parts[3], pool_index * feature_count, feature_count, 1)
    merged_inner = jnp.concatenate(
        [
            combine_adapter_weight(frozen_query_weight, factor_aq, factor_bq),
            combine_adapter_weight(frozen_key_weight, factor_ak, factor_bk),
            combine_adapter_weight(frozen_value_weight, factor_av, factor_bv),
        ],
        1,
    )
    combined_output_weight = combine_adapter_weight(frozen_output_weight, factor_ao, factor_bo)
    states = incoming_hidden.astype(jnp.float32)
    normed = (
        states
        * lax.rsqrt(jnp.mean(states * states, -1, keepdims=True) + norm_eps)
        * attention_norm_gain.astype(jnp.float32)
    )
    normed = jnp.transpose(normed.astype(jnp.bfloat16), (1, 0, 2))
    rows_dev = filled_lengths.shape[0]
    steps_count = incoming_hidden.shape[0]
    kv_local = earlier_keys.shape[2]
    head_dim = earlier_keys.shape[3]
    query_local = query_cols // head_dim
    all_steps = jnp.arange(steps_count)
    spread = lax.all_to_all(normed, "pool", split_axis=2, concat_axis=0, tiled=True)
    projected = lax.psum_scatter(
        jnp.einsum("rnd,dc->rnc", spread, merged_inner, preferred_element_type=jnp.float32),
        "pool",
        scatter_dimension=0,
        tiled=True,
    )
    positions = (filled_lengths[:, None] + all_steps[None, :]).astype(jnp.float32)[:, :, None]
    query_part = projected[..., :query_cols].reshape(rows_dev, steps_count, query_local, head_dim)
    key_part = projected[..., query_cols : query_cols + key_cols].reshape(
        rows_dev, steps_count, kv_local, head_dim
    )
    value_part = projected[..., query_cols + key_cols :].reshape(
        rows_dev, steps_count, kv_local, head_dim
    )
    queries = rotate(query_part, positions).astype(jnp.bfloat16)
    fresh_keys = rotate(key_part, positions).astype(jnp.bfloat16)
    fresh_values = value_part.astype(jnp.bfloat16)
    head_rows = attend(
        queries, earlier_keys, earlier_values, fresh_keys, fresh_values, filled_lengths, all_steps
    )
    partial_out = jnp.einsum(
        "rnk,kd->nrd",
        lax.all_gather(head_rows, "pool", axis=0, tiled=True),
        combined_output_weight,
        preferred_element_type=jnp.float32,
    )
    result = lax.psum(partial_out, "tensor").astype(jnp.bfloat16)
    return result


def solution(mesh):
    in_specs = (
        P(None, ("groups", "pool"), None),
        P(),
        P("pool", "tensor"),
        P("pool", "tensor"),
        P("pool", "tensor"),
        P("tensor", "pool"),
        P("groups", "pool"),
        P(("groups", "pool"), None),
        P("groups", "pool"),
        P(("groups", "pool"), None),
        P("groups", "pool"),
        P(("groups", "pool"), None),
        P("groups", "pool"),
        P(("groups", "pool"), None),
        P(("groups", "pool"), None, "tensor", None),
        P(("groups", "pool"), None, "tensor", None),
        P(("groups", "pool")),
    )
    out_specs = P(None, "groups", "pool")
    return jax.shard_map(
        on_device, mesh=mesh, in_specs=in_specs, out_specs=out_specs, check_vma=False
    )
```

profile of v0, /device:TPU:0, one launch (start us, length us, event | category | flops | bytes accessed | tf_op | source)
XLA Modules:
  0.0 275.5 jit_solution(14356270754320371514)
XLA Ops:
  6.5 0.7 all-gather.17.cloned.1.call-update
  7.3 0.7 all-gather.15.cloned.1.call-update
  9.3 0.7 convert_element_type.99
  10.0 1.0 fusion.32
  11.1 0.9 fusion.35
  12.0 6.9 %copy.47 = bf16[1,4,8192]{1,0,2:T(2,128)(2,1)} copy(bf16[1,4,8192]{2,1,0:T(4,128)(2,1)S(1)} %fusion.35) | data formatting | bytes 131072 | tf_op jit(solution)/shard_map/transpose | solution.py:132
  19.4 46.5 %reduce.5 = bf16[8192,4]{1,0:T(8,128)(2,1)} reduce(bf16[8192,1,4]{2,1,0:T(2,128)(2,1)} %bitcast.93, bf16[]{:T(256)} %broadcast.122), dimensions={1}, to_apply=%bitcast.83.reduce_sub_computation | reduce | bytes 131074
  65.9 5.6 %reshape.263 = bf16[4,2,4096]{2,1,0:T(2,128)(2,1)} reshape(bf16[8192,4]{1,0:T(8,128)(2,1)} %reduce.5) | data formatting | bytes 131072
  71.5 6.3 %all-to-all-start = ((bf16[4,2,4096]{2,1,0:T(2,128)(2,1)}), bf16[4,2,4096]{2,1,0:T(2,128)(2,1)S(1)}, u32[]{:S(2)}, u32[]{:S(2)}) async-start(bf16[4,2,4096]{2,1,0:T(2,128)(2,1)} %reshape.263), calls=%async_computation | async-start | bytes 131072 | tf_op jit(solution)/shard_map/all_to_all | solution.py:139
  77.8 1.5 copy.52
  79.3 2.3 copy.51
  81.6 12.2 %copy.50 = bf16[2048,2048]{0,1:T(8,128)(2,1)} copy(bf16[2048,2048]{1,0:T(8,128)(2,1)} %param.19) | data formatting | bytes 16777216 | tf_op args[2]
  93.8 14.0 %all_gather.34 = bf16[64,1024]{1,0:T(8,128)(2,1)S(1)} all-gather(bf16[16,1024]{1,0:T(8,128)(2,1)S(1)} %copy-done.3), channel_id=1, replica_groups=mesh['groups'=2,'pool'=4,'tensor'=4] {'pool'}, dimensions={0}, use_global_device_ids=true | all-gather | bytes 163840 | tf_op jit(solution)/shard_map/all_gather | solution.py:100
  107.8 14.4 %all_gather.32 = bf16[64,1024]{1,0:T(8,128)(2,1)S(1)} all-gather(bf16[16,1024]{1,0:T(8,128)(2,1)S(1)} %copy-done.4), channel_id=1, replica_groups=mesh['groups'=2,'pool'=4,'tensor'=4] {'pool'}, dimensions={0}, use_global_device_ids=true | all-gather | bytes 163840 | tf_op jit(solution)/shard_map/all_gather | solution.py:99
  122.2 6.1 %reshape.264 = bf16[8192,1,4]{2,1,0:T(2,128)(2,1)} reshape(bf16[4,2,4096]{2,1,0:T(2,128)(2,1)S(1)} %all-to-all-done) | data formatting | bytes 131072
  128.3 8.1 %copy.48 = bf16[1,4,8192]{2,1,0:T(4,128)(2,1)S(1)} copy(bf16[1,4,8192]{1,0,2:T(2,128)(2,1)} %bitcast.94) | data formatting | bytes 131072 | tf_op jit(solution)/shard_map/all_to_all | solution.py:139
  136.4 2.5 fusion.7
  138.9 2.8 %fusion.6 = bf16[2048,256]{0,1:T(8,128)(2,1)} fusion(bf16[2048,256]{0,1:T(8,128)(2,1)} %copy.51, bf16[8192,64]{0,1:T(8,128)(2,1)} %all-gather.15.cloned.1.call-done, s32[]{:T(128)S(6)} %select_n.26, bf16[64,1024]{1,0:T(8,128)(2,1)S(1)} %all_gather.32, s32[]{:T(128)S(6)} %select_n.27), kind=kOutput, calls=%fused_computation.12 | convolution fusion | flops 68681728 | bytes 2392072 | tf_op jit(solution)/shard_map/dot_general | solution.py:25
  141.7 6.1 %add_convert_fusion = bf16[2048,2048]{0,1:T(8,128)(2,1)S(1)} fusion(bf16[2048,2048]{0,1:T(8,128)(2,1)} %copy.50, bf16[64,8192]{1,0:T(8,128)(2,1)} %all-gather.13.cloned.1.call-done, s32[]{:T(128)S(6)} %select_n.25, bf16[8192,64]{0,1:T(8,128)(2,1)} %all-gather.11.cloned.1.call-done, s32[]{:T(128)S(6)} %select_n.26), kind=kOutput, calls=%fused_computation | convolution fusion | flops 549453824 | bytes 17301512 | tf_op jit(solution)/shard_map/dot_general | solution.py:25
  147.8 4.7 %fusion = f32[4,4,2560]{2,1,0:T(4,128)} fusion(bf16[4,4,2048]{2,1,0:T(4,128)(2,1)S(1)} %bitcast.95, bf16[2048,256]{0,1:T(8,128)(2,1)S(1)} %copy-done.1, bf16[2048,256]{0,1:T(8,128)(2,1)S(1)} %copy-done.2, bf16[2048,2048]{0,1:T(8,128)(2,1)S(1)} %add_convert_fusion), kind=kOutput, calls=%fused_computation.3 | convolution fusion | flops 199229440 | bytes 10715136 | tf_op jit(solution)/shard_map/rnd,dc->rnc/dot_general | solution.py:141
  153.2 0.7 all-gather.7.cloned.1.call-update
  155.3 33.5 %all-reduce.4.cloned.1.call-done = f32[4,4,2560]{2,1,0:T(4,128)} async-done(((f32[4,4,2560]{2,1,0:T(4,128)}), f32[4,4,2560]{2,1,0:T(4,128)}) %all-reduce.4.cloned.1.call-update) | async-done | bytes 163856
  188.7 1.4 dynamic-slice_bitcast_fusion.1
  190.2 1.4 dynamic-slice_bitcast_fusion
  192.0 0.9 fusion.59
  193.3 2.1 fusion.14
  195.5 1.5 fusion.18
  197.0 13.5 %all_gather.35 = bf16[4,4,2048]{2,1,0:T(4,128)(2,1)S(1)} all-gather(bf16[1,4,2048]{2,1,0:T(4,128)(2,1)S(1)} %convert_element_type.115), channel_id=1, replica_groups=mesh['groups'=2,'pool'=4,'tensor'=4] {'pool'}, dimensions={0}, use_global_device_ids=true | all-gather | bytes 81920 | tf_op jit(solution)/shard_map/all_gather | solution.py:162
  210.5 8.2 %all-gather.9.cloned.1.call-done = bf16[64,8192]{1,0:T(8,128)(2,1)} async-done(((bf16[16,8192]{1,0:T(8,128)(2,1)}), bf16[64,8192]{1,0:T(8,128)(2,1)}) %all-gather.9.cloned.1.call-update) | async-done | bytes 1048592 | tf_op jit(solution)/shard_map/all_gather | solution.py:101
  218.7 29.2 %all-gather.7.cloned.1.call-done = bf16[8192,64]{0,1:T(8,128)(2,1)} async-done(((bf16[8192,16]{0,1:T(8,128)(2,1)}), bf16[8192,64]{0,1:T(8,128)(2,1)}) %all-gather.7.cloned.1.call-update) | async-done | bytes 1048592 | tf_op jit(solution)/shard_map/all_gather | solution.py:95
  247.9 7.3 %fusion.8 = f32[4,4,2048]{2,0,1:T(4,128)S(1)} fusion(bf16[4,4,2048]{2,1,0:T(4,128)(2,1)S(1)} %all_gather.35, bf16[2048,2048]{1,0:T(8,128)(2,1)} %param.22, bf16[64,8192]{1,0:T(8,128)(2,1)} %all-gather.9.cloned.1.call-done, s32[]{:T(128)S(6)} %select_n.26, bf16[8192,64]{0,1:T(8,128)(2,1)} %all-gather.7.cloned.1.call-done, s32[]{:T(128)S(6)} %select_n.25), kind=kOutput, calls=%fused_computation.14 | convolution fusion | flops 683671552 | bytes 9109512 | tf_op jit(solution)/shard_map/rnk,kd->nrd/dot_general | solution.py:160
  255.2 12.8 %all-reduce.5 = bf16[4,4,2048]{2,0,1:T(4,128)(2,1)S(1)} all-reduce(f32[4,4,2048]{2,0,1:T(4,128)S(1)} %fusion.8), channel_id=1, replica_groups=mesh['groups'=2,'pool'=4,'tensor'=4] {'tensor'}, use_global_device_ids=true, to_apply=%region_6.7 | all-reduce | flops 32768 | bytes 196608 | tf_op jit(solution)/shard_map/psum | solution.py:166
  (47 shorter events, 4.7 us)
Async XLA Ops:
  6.5 185.5 %copy-start = (bf16[1,4096,2,128]{3,2,1,0:T(2,128)(2,1)S(1)}, bf16[1,4096,2,128]{3,2,1,0:T(2,128)(2,1)}, u32[]{:S(2)}) copy-start(bf16[1,4096,2,128]{3,2,1,0:T(2,128)(2,1)} %param.31) | copy-start | bytes 6291460
  6.5 129.9 %all-gather.17.cloned.1.call-start = ((), (), s32[]{:S(2)}) async-start(), calls=%async_computation.6 | async-start | bytes 1310720 | tf_op jit(solution)/shard_map/all_gather | solution.py:94
  7.3 131.7 %all-gather.15.cloned.1.call-start = ((), (), s32[]{:S(2)}) async-start(), calls=%async_computation.5 | async-start | bytes 1310720 | tf_op jit(solution)/shard_map/all_gather | solution.py:93
  8.0 133.7 %all-gather.13.cloned.1.call-start = ((), (), s32[]{:S(2)}) async-start(), calls=%async_computation.4 | async-start | bytes 1310720 | tf_op jit(solution)/shard_map/all_gather | solution.py:98
  8.7 133.0 %all-gather.11.cloned.1.call-start = ((), (), s32[]{:S(2)}) async-start(), calls=%async_computation.3 | async-start | bytes 1310720 | tf_op jit(solution)/shard_map/all_gather | solution.py:92
  71.5 50.7 %all-to-all-start = ((bf16[4,2,4096]{2,1,0:T(2,128)(2,1)}), bf16[4,2,4096]{2,1,0:T(2,128)(2,1)S(1)}, u32[]{:S(2)}, u32[]{:S(2)}) async-start(bf16[4,2,4096]{2,1,0:T(2,128)(2,1)} %reshape.263), calls=%async_computation | async-start | bytes 131072 | tf_op jit(solution)/shard_map/all_to_all | solution.py:139
  77.8 110.9 %all-reduce.4.cloned.1.call-start = ((), (), s32[]{:S(2)}) async-start(), calls=%async_computation.7 | async-start | bytes 327680
  81.6 12.2 %copy-start.3 = (bf16[16,1024]{1,0:T(8,128)(2,1)S(1)}, bf16[16,1024]{1,0:T(8,128)(2,1)}, u32[]{:S(2)}) copy-start(bf16[16,1024]{1,0:T(8,128)(2,1)} %param.28) | copy-start | bytes 98308
  81.6 26.2 %copy-start.4 = (bf16[16,1024]{1,0:T(8,128)(2,1)S(1)}, bf16[16,1024]{1,0:T(8,128)(2,1)}, u32[]{:S(2)}) copy-start(bf16[16,1024]{1,0:T(8,128)(2,1)} %param.26) | copy-start | bytes 98308
  141.7 6.1 %copy-start.1 = (bf16[2048,256]{0,1:T(8,128)(2,1)S(1)}, bf16[2048,256]{0,1:T(8,128)(2,1)}, u32[]{:S(2)}) copy-start(bf16[2048,256]{0,1:T(8,128)(2,1)} %fusion.7) | copy-start | bytes 3145732
  141.7 6.1 %copy-start.2 = (bf16[2048,256]{0,1:T(8,128)(2,1)S(1)}, bf16[2048,256]{0,1:T(8,128)(2,1)}, u32[]{:S(2)}) copy-start(bf16[2048,256]{0,1:T(8,128)(2,1)} %fusion.6) | copy-start | bytes 3145732
  147.8 6.8 %copy-start.5 = (u32[32]{0:T(128)S(1)}, u32[32]{0:T(128)}, u32[]{:S(2)}) copy-start(u32[32]{0:T(128)} %constant.44) | copy-start | bytes 388
  152.5 66.2 %all-gather.9.cloned.1.call-start = ((), (), s32[]{:S(2)}) async-start(), calls=%async_computation.2 | async-start | bytes 1310720 | tf_op jit(solution)/shard_map/all_gather | solution.py:101
  153.1 94.8 %all-gather.7.cloned.1.call-start = ((), (), s32[]{:S(2)}) async-start(), calls=%async_computation.1 | async-start | bytes 1310720 | tf_op jit(solution)/shard_map/all_gather | solution.py:95
Sparse Core Ops, SparseCore 0:
  8.9 30.6 all-gather.16
  41.2 27.4 all-gather.14
  70.2 29.6 all-gather.12
  101.3 28.5 all-gather.10
  152.7 36.0 all-reduce.3
  190.2 28.4 all-gather.8
  220.4 27.4 all-gather.6
where the time goes:
time: 277 us; the launch traced here: 275 us
  waiting for transfers between devices  74.7 us (27%)
  blocking collectives  54.6 us (20%)
  other arithmetic  49.9 us (18%)
  local copies, waits for them, and re-layouts  47.2 us (17%)
  matrix products  28.2 us (10%)
  between operations  14.3 us (5%)
  starting transfers between devices  6.51 us (2%)
    unnamed x1, other arithmetic  46.5 us
    unnamed x8, waiting for transfers between devices  37.3 us
    unnamed x21, local copies, waits for them, and re-layouts  30.1 us
    all_gather x1, waiting for transfers between devices, on_device(): lax.all_gather(output_adapter_first, 'pool', axis=1, tiled=True)  29.2 us
    all_gather x1, blocking collectives, on_device(): lax.all_gather(key_adapter_second, 'pool', axis=0, tiled=True)  14.4 us
    all_gather x1, blocking collectives, on_device(): lax.all_gather(value_adapter_second, 'pool', axis=0, tiled=True)  14 us
    all_gather x1, blocking collectives, on_device(): lax.all_gather(head_rows, 'pool', axis=0, tiled=True)  13.5 us
    psum x1, blocking collectives, on_device(): result = lax.psum(partial_out, 'tensor').astype(jnp.bfloat16)  12.8 us
  transfers between devices with their start and end apart: 8, of which 3 were waited for; matrix products, arithmetic and copies ran while one was open for 39% of the time, Pallas kernels for 0%

commit v1 on v0

--- a/solution.py
+++ b/solution.py
@@ -1,10 +1,16 @@
+import functools
+import math
+
 import jax
 import jax.numpy as jnp
 from jax import lax
+from jax.experimental import pallas as pl
+from jax.experimental.pallas import tpu as pltpu
 from jax.sharding import PartitionSpec as P
 
 rope_base = 500000.0
 norm_eps = 1e-05
+MESH = pl.DeviceIdType.MESH
 
 
 def rotate(values, positions):
@@ -167,6 +173,509 @@
     return result
 
 
+def layer_kernel(
+    pool,
+    tensor,
+    steps,
+    kv_heads,
+    x_ref,
+    gain_ref,
+    freq_ref,
+    len_ref,
+    wq_hbm,
+    wk_hbm,
+    wv_hbm,
+    wo_hbm,
+    aq_hbm,
+    bq_hbm,
+    ak_hbm,
+    bk_hbm,
+    av_hbm,
+    bv_hbm,
+    ao_hbm,
+    bo_hbm,
+    keys_hbm,
+    vals_hbm,
+    out_ref,
+    w_in,
+    w_out,
+    keys,
+    vals,
+    a_in,
+    b_in,
+    a_out,
+    b_out,
+    a_cols,
+    x_send,
+    x_recv,
+    x_full,
+    proj,
+    rs_send,
+    rs_recv,
+    scores,
+    h_send,
+    h_recv,
+    h_full,
+    part,
+    o_recv,
+    fin,
+    w_sem,
+    own_sem,
+    send_sem,
+    recv_sem,
+    t_send_sem,
+    t_recv_sem,
+):
+    f32, bf16 = jnp.float32, jnp.bfloat16
+    me = lax.axis_index("pool")
+    ten = lax.axis_index("tensor")
+    rank = aq_hbm.shape[0]
+    depth, q_cols = wq_hbm.shape
+    kv_cols = wk_hbm.shape[1]
+    in_cols = q_cols + 2 * kv_cols
+    o_rows, o_cols = wo_hbm.shape
+    head = keys_hbm.shape[1]
+    q_heads = q_cols // head
+    group = q_heads // kv_heads
+    tokens = pool * steps
+
+    def at_block(index, size):
+        return pl.ds(pl.multiple_of(index * size, size), size)
+
+    def peer(off, axis, size):
+        here = me if axis == "pool" else ten
+        return lax.rem(here + off, size), lax.rem(here + size - off, size)
+
+    loads = [
+        pltpu.make_async_copy(wq_hbm, w_in.at[:, pl.ds(0, q_cols)], w_sem.at[0]),
+        pltpu.make_async_copy(wk_hbm, w_in.at[:, pl.ds(q_cols, kv_cols)], w_sem.at[1]),
+        pltpu.make_async_copy(wv_hbm, w_in.at[:, pl.ds(q_cols + kv_cols, kv_cols)], w_sem.at[2]),
+        pltpu.make_async_copy(wo_hbm, w_out, w_sem.at[3]),
+        pltpu.make_async_copy(keys_hbm, keys, w_sem.at[4]),
+        pltpu.make_async_copy(vals_hbm, vals, w_sem.at[5]),
+    ]
+
+    def pieces(dst, src):
+        rows = at_block(src, rank)
+        return [
+            (aq_hbm.at[:, at_block(dst, depth)], a_in.at[0, rows, :]),
+            (bq_hbm.at[:, at_block(ten, q_cols)], b_in.at[rows, pl.ds(0, q_cols)]),
+            (ak_hbm.at[:, at_block(dst, depth)], a_in.at[1, rows, :]),
+            (bk_hbm.at[:, at_block(ten, kv_cols)], b_in.at[rows, pl.ds(q_cols, kv_cols)]),
+            (av_hbm.at[:, at_block(dst, depth)], a_in.at[2, rows, :]),
+            (
+                bv_hbm.at[:, at_block(ten, kv_cols)],
+                b_in.at[rows, pl.ds(q_cols + kv_cols, kv_cols)],
+            ),
+            (ao_hbm.at[:, at_block(ten, o_rows)], a_out.at[rows, :]),
+            (bo_hbm.at[:, at_block(dst, o_cols)], b_out.at[rows, :]),
+        ]
+
+    own = [
+        pltpu.make_async_copy(src, dst, own_sem.at[i])
+        for i, (src, dst) in enumerate(pieces(me, me))
+    ]
+    for copy in own[:6] + loads[:3]:
+        copy.start()
+
+    barrier = pltpu.get_barrier_semaphore()
+    for off in range(1, pool):
+        pl.semaphore_signal(
+            barrier, inc=1, device_id={"pool": peer(off, "pool", pool)[0]}, device_id_type=MESH
+        )
+    for off in range(1, tensor):
+        pl.semaphore_signal(
+            barrier,
+            inc=1,
+            device_id={"tensor": peer(off, "tensor", tensor)[0]},
+            device_id_type=MESH,
+        )
+
+    fold = 16 // steps
+    states = x_ref[...].astype(f32)
+    mean = jnp.mean(states * states, -1, keepdims=True)
+    normed = states * lax.rsqrt(mean + norm_eps) * gain_ref[...].astype(f32)
+    width = depth // fold
+    for dst in range(pool):
+        folded = jnp.concatenate(
+            [normed[:, dst * depth + i * width : dst * depth + (i + 1) * width] for i in range(fold)],
+            0,
+        )
+        x_send[dst] = folded.astype(bf16)
+    pl.semaphore_wait(barrier, pool + tensor - 2)
+
+    def to_pool(kind, off, src, dst_ref):
+        return pltpu.make_async_remote_copy(
+            src_ref=src,
+            dst_ref=dst_ref,
+            send_sem=send_sem.at[kind, off],
+            recv_sem=recv_sem.at[kind, off],
+            device_id={"pool": peer(off, "pool", pool)[0]},
+            device_id_type=MESH,
+        )
+
+    def sends(off):
+        dst, _ = peer(off, "pool", pool)
+        out = [to_pool(i, off, a, b) for i, (a, b) in enumerate(pieces(dst, me))]
+        return out + [to_pool(8, off, x_send.at[dst], x_recv.at[me])]
+
+    def arrivals(off):
+        _, src = peer(off, "pool", pool)
+        out = [to_pool(i, off, b, b) for i, (a, b) in enumerate(pieces(me, src))]
+        return out + [to_pool(8, off, x_recv.at[src], x_recv.at[src])]
+
+    offs = list(range(1, pool))
+    sent = {off: sends(off) for off in offs}
+    come = {off: arrivals(off) for off in offs}
+    for kind in (8, 0, 1, 2, 3, 4, 5, 6, 7):
+        for off in offs:
+            sent[off][kind].start()
+    for copy in own[6:] + loads[3:]:
+        copy.start()
+
+    def wait_kinds(kinds):
+        for kind in kinds:
+            if kind < 8:
+                own[kind].wait()
+            for off in offs:
+                come[off][kind].wait_recv()
+
+    x_recv[me] = x_send[me]
+    wait_kinds((8,))
+    rows = []
+    for src in range(pool):
+        got = x_recv[src].astype(f32)
+        rows.append(
+            jnp.concatenate([got[i * steps : (i + 1) * steps, :] for i in range(fold)], 1)
+        )
+    x_full[...] = jnp.concatenate(rows, 0).astype(bf16)
+
+    tile = 256
+    chunk = min(512, depth)
+
+    def merged(a_tall, row0, b_ref, w_ref, column):
+        low_rank = jnp.dot(
+            a_tall[pl.ds(row0, chunk), :], b_ref[:, column], preferred_element_type=f32
+        )
+        return (w_ref[pl.ds(row0, chunk), column].astype(f32) + low_rank).astype(bf16)
+
+    def project(which, first, count):
+        a_cols[...] = a_in[which].T
+
+        def one(j, carry):
+            column = pl.ds(pl.multiple_of(first + j * tile, tile), tile)
+            total = jnp.zeros((tokens, tile), f32)
+            for row0 in range(0, depth, chunk):
+                block = merged(a_cols, row0, b_in, w_in, column)
+                total += jnp.dot(
+                    x_full[:, row0 : row0 + chunk], block, preferred_element_type=f32
+                )
+            proj[:, column] = total
+            return carry
+
+        lax.fori_loop(0, count // tile, one, 0)
+
+    wait_kinds((0, 1))
+    loads[0].wait()
+    project(0, 0, q_cols)
+    wait_kinds((2, 3))
+    loads[1].wait()
+    project(1, q_cols, kv_cols)
+    wait_kinds((4, 5))
+    loads[2].wait()
+    project(2, q_cols + kv_cols, kv_cols)
+
+    half = in_cols // 2
+    for dst in range(pool):
+        mine = proj[dst * steps : (dst + 1) * steps, :]
+        rs_send[dst] = jnp.concatenate([mine[:, :half], mine[:, half:]], 0)
+    rs_sent, rs_come = [], []
+    for off in offs:
+        dst, src = peer(off, "pool", pool)
+        copy = to_pool(9, off, rs_send.at[dst], rs_recv.at[me])
+        copy.start()
+        rs_sent.append(copy)
+        rs_come.append(to_pool(9, off, rs_recv.at[src], rs_recv.at[src]))
+    rs_recv[me] = rs_send[me]
+
+    wait_kinds((6, 7))
+    loads[3].wait()
+    a_cols[...] = a_out[...].T
+
+    def merge_out(j, carry):
+        column = pl.ds(pl.multiple_of(j * tile, tile), tile)
+        for row0 in range(0, o_rows, chunk):
+            w_out[pl.ds(row0, chunk), column] = merged(a_cols, row0, b_out, w_out, column)
+        return carry
+
+    lax.fori_loop(0, o_cols // tile, merge_out, 0)
+
+    for copy in rs_come:
+        copy.wait_recv()
+    summed = rs_recv[0]
+    for src in range(1, pool):
+        summed = summed + rs_recv[src]
+    flat = jnp.concatenate([summed[:steps], summed[steps:]], 1)
+
+    length = len_ref[0]
+    lanes = freq_ref.shape[1]
+    spare = freq_ref.shape[0]
+    step_of = lax.rem(lax.broadcasted_iota(jnp.int32, (spare, lanes), 0), steps)
+    angles = (length + step_of).astype(f32) * freq_ref[...]
+    cosine = jnp.cos(angles)
+    lane = lax.broadcasted_iota(jnp.int32, (spare, lanes), 1)
+    sine = jnp.where(lane < head // 2, -jnp.sin(angles), jnp.sin(angles))
+
+    def stack(first, count):
+        return jnp.concatenate(
+            [flat[:, first + h * head : first + (h + 1) * head] for h in range(count)], 0
+        )
+
+    def turned(values):
+        turns = values.shape[0] // spare
+        cos_all = jnp.concatenate([cosine] * turns, 0)
+        sin_all = jnp.concatenate([sine] * turns, 0)
+        return (values * cos_all + pltpu.roll(values, head // 2, 1) * sin_all).astype(bf16)
+
+    queries = turned(stack(0, q_heads))
+    fresh_keys = turned(stack(q_cols, kv_heads))
+    fresh_values = stack(q_cols + kv_cols, kv_heads).astype(bf16)
+
+    scale = 1.0 / math.sqrt(head)
+    q_rows = q_heads * steps
+    span = 1024
+    spans = keys.shape[0] // span
+    row_head = lax.broadcasted_iota(jnp.int32, (q_rows, 1), 0) // (group * steps)
+    row_step = lax.rem(lax.broadcasted_iota(jnp.int32, (q_rows, 1), 0), steps)
+    nt = (((1,), (1,)), ((), ()))
+    fresh_col = lax.broadcasted_iota(jnp.int32, (1, kv_heads * steps), 1)
+    fresh_seen = (fresh_col // steps == row_head) & (lax.rem(fresh_col, steps) <= row_step)
+    fresh_scores = jnp.where(
+        fresh_seen,
+        lax.dot_general(queries, fresh_keys, nt, preferred_element_type=f32) * scale,
+        -1e30,
+    )
+    loads[4].wait()
+
+    def score(j, top):
+        at = pl.ds(pl.multiple_of(j * span, span), span)
+        column = lax.broadcasted_iota(jnp.int32, (1, span), 1) + j * span
+        slot = column // kv_heads
+        slot_head = jnp.where(slot < length, lax.rem(column, kv_heads), -1)
+        value = lax.dot_general(queries, keys[at, :], nt, preferred_element_type=f32) * scale
+        value = jnp.where(slot_head == row_head, value, -1e30)
+        scores[:, at] = value
+        for i in range(0, span, 128):
+            top = jnp.maximum(top, value[:, i : i + 128])
+        return top
+
+    top = lax.fori_loop(0, spans, score, jnp.full((q_rows, 128), -1e30, f32))
+    top = jnp.maximum(
+        jnp.max(top, 1, keepdims=True), jnp.max(fresh_scores, 1, keepdims=True)
+    )
+
+    def expo(j, total):
+        at = pl.ds(pl.multiple_of(j * span, span), span)
+        value = jnp.exp(scores[:, at] - top)
+        scores[:, at] = value
+        for i in range(0, span, 128):
+            total = total + value[:, i : i + 128]
+        return total
+
+    total = lax.fori_loop(0, spans, expo, jnp.zeros((q_rows, 128), f32))
+    fresh_exp = jnp.exp(fresh_scores - top)
+    inverse = 1.0 / (
+        jnp.sum(total, 1, keepdims=True) + jnp.sum(fresh_exp, 1, keepdims=True)
+    )
+    loads[5].wait()
+
+    def mix(j, acc):
+        at = pl.ds(pl.multiple_of(j * span, span), span)
+        weights = (scores[:, at] * inverse).astype(bf16)
+        return acc + jnp.dot(weights, vals[at, :], preferred_element_type=f32)
+
+    mixed = jnp.dot(
+        (fresh_exp * inverse).astype(bf16), fresh_values, preferred_element_type=f32
+    )
+    mixed = lax.fori_loop(0, spans, mix, mixed)
+    h_send[...] = mixed.astype(bf16)
+
+    h_sent, h_come = [], []
+    for off in offs:
+        _, src = peer(off, "pool", pool)
+        copy = to_pool(10, off, h_send, h_recv.at[me])
+        copy.start()
+        h_sent.append(copy)
+        h_come.append(to_pool(10, off, h_recv.at[src], h_recv.at[src]))
+    h_recv[me] = h_send[...]
+    for copy in h_come:
+        copy.wait_recv()
+    every = [h_recv[src].astype(f32) for src in range(pool)]
+    for h in range(q_heads):
+        h_full[:, h * head : (h + 1) * head] = jnp.concatenate(
+            [rows_of[h * steps : (h + 1) * steps] for rows_of in every], 0
+        ).astype(bf16)
+
+    def output(j, carry):
+        column = pl.ds(pl.multiple_of(j * tile, tile), tile)
+        part[:, column] = jnp.dot(h_full[...], w_out[:, column], preferred_element_type=f32)
+        return carry
+
+    lax.fori_loop(0, o_cols // tile, output, 0)
+
+    share = o_cols // tensor
+
+    def to_tensor(kind, off, src, dst_ref):
+        return pltpu.make_async_remote_copy(
+            src_ref=src,
+            dst_ref=dst_ref,
+            send_sem=t_send_sem.at[kind, off],
+            recv_sem=t_recv_sem.at[kind, off],
+            device_id={"tensor": peer(off, "tensor", tensor)[0]},
+            device_id_type=MESH,
+        )
+
+    t_offs = list(range(1, tensor))
+    o_sent, o_come = [], []
+    for off in t_offs:
+        dst, src = peer(off, "tensor", tensor)
+        copy = to_tensor(0, off, part.at[:, at_block(dst, share)], o_recv.at[ten])
+        copy.start()
+        o_sent.append(copy)
+        o_come.append(to_tensor(0, off, o_recv.at[src], o_recv.at[src]))
+    o_recv[ten] = part[:, at_block(ten, share)]
+    for copy in o_come:
+        copy.wait_recv()
+    done = o_recv[0]
+    for src in range(1, tensor):
+        done = done + o_recv[src]
+    done = jnp.concatenate(
+        [done[r * steps + s : r * steps + s + 1] for s in range(steps) for r in range(pool)], 0
+    )
+    fin[ten] = done.astype(bf16)
+    f_sent, f_come = [], []
+    for off in t_offs:
+        _, src = peer(off, "tensor", tensor)
+        copy = to_tensor(1, off, fin.at[ten], fin.at[ten])
+        copy.start()
+        f_sent.append(copy)
+        f_come.append(to_tensor(1, off, fin.at[src], fin.at[src]))
+    for copy in f_come:
+        copy.wait_recv()
+    for src in range(tensor):
+        out_ref[:, src * share : (src + 1) * share] = fin[src]
+    for off in offs:
+        for copy in sent[off]:
+            copy.wait_send()
+    for copy in rs_sent + h_sent + o_sent + f_sent:
+        copy.wait_send()
+
+
+def fits(pool, tensor, args):
+    hidden, wq, wk, wo = args[0], args[2], args[3], args[5]
+    rank, keys = args[7].shape[0], args[14]
+    steps = hidden.shape[0]
+    return (
+        keys.shape[0] == 1
+        and keys.shape[3] == 128
+        and rank % 16 == 0
+        and pool > 1
+        and tensor > 1
+        and pool * steps == 16
+        and steps == 4
+        and (keys.shape[2] * steps) % 8 == 0
+        and wq.shape[0] % 512 == 0
+        and wq.shape[1] % 256 == 0
+        and wk.shape[1] % 256 == 0
+        and wo.shape[0] == wq.shape[0]
+        and wo.shape[1] % (128 * tensor) == 0
+        and wo.shape[1] % 256 == 0
+        and (keys.shape[1] * keys.shape[2]) % 1024 == 0
+        and wq.shape[0] * (wq.shape[1] + 2 * wk.shape[1] + wo.shape[1]) <= 12 * 1024 * 1024
+    )
+
+
+def on_device_fused(pool, tensor, *args):
+    if not fits(pool, tensor, args):
+        return on_device(*args)
+    f32, bf16 = jnp.float32, jnp.bfloat16
+    hidden, gain, wq, wk, wv, wo, aq, bq, ak, bk, av, bv, ao, bo, keys, vals, lengths = args
+    steps = hidden.shape[0]
+    kv_heads, head = keys.shape[2:]
+    rank = bq.shape[0]
+    depth, q_cols = wq.shape
+    in_cols = q_cols + 2 * wk.shape[1]
+    o_rows, o_cols = wo.shape
+    q_rows = q_cols // head * steps
+    slots = keys.shape[1] * kv_heads
+    tokens = pool * steps
+    half = jnp.arange(head // 2, dtype=f32)
+    frequency = rope_base ** (-(half * 2.0 / head))
+    freq = jnp.broadcast_to(jnp.concatenate([frequency, frequency])[None, :], (8, head))
+    vmem = pl.BlockSpec(memory_space=pltpu.VMEM)
+    hbm = pl.BlockSpec(memory_space=pl.ANY)
+    share = o_cols // tensor
+    out = pl.pallas_call(
+        functools.partial(layer_kernel, pool, tensor, steps, kv_heads),
+        out_shape=jax.ShapeDtypeStruct((tokens, o_cols), bf16),
+        in_specs=[vmem, vmem, vmem, pl.BlockSpec(memory_space=pltpu.SMEM)] + [hbm] * 14,
+        out_specs=vmem,
+        scratch_shapes=[
+            pltpu.VMEM((depth, in_cols), bf16),
+            pltpu.VMEM((o_rows, o_cols), bf16),
+            pltpu.VMEM((slots, head), bf16),
+            pltpu.VMEM((slots, head), bf16),
+            pltpu.VMEM((3, pool * rank, depth), bf16),
+            pltpu.VMEM((pool * rank, in_cols), bf16),
+            pltpu.VMEM((pool * rank, o_rows), bf16),
+            pltpu.VMEM((pool * rank, o_cols), bf16),
+            pltpu.VMEM((depth, pool * rank), bf16),
+            pltpu.VMEM((pool, 16, depth * steps // 16), bf16),
+            pltpu.VMEM((pool, 16, depth * steps // 16), bf16),
+            pltpu.VMEM((tokens, depth), bf16),
+            pltpu.VMEM((tokens, in_cols), f32),
+            pltpu.VMEM((pool, 2 * steps, in_cols // 2), f32),
+            pltpu.VMEM((pool, 2 * steps, in_cols // 2), f32),
+            pltpu.VMEM((q_rows, slots), f32),
+            pltpu.VMEM((q_rows, head), bf16),
+            pltpu.VMEM((pool, q_rows, head), bf16),
+            pltpu.VMEM((tokens, o_rows), bf16),
+            pltpu.VMEM((tokens, o_cols), f32),
+            pltpu.VMEM((tensor, tokens, share), f32),
+            pltpu.VMEM((tensor, tokens, share), bf16),
+            pltpu.SemaphoreType.DMA((6,)),
+            pltpu.SemaphoreType.DMA((8,)),
+            pltpu.SemaphoreType.DMA((11, pool)),
+            pltpu.SemaphoreType.DMA((11, pool)),
+            pltpu.SemaphoreType.DMA((2, tensor)),
+            pltpu.SemaphoreType.DMA((2, tensor)),
+        ],
+        compiler_params=pltpu.CompilerParams(
+            collective_id=0, has_side_effects=True, vmem_limit_bytes=56 * 1024 * 1024
+        ),
+    )(
+        hidden.reshape(steps, hidden.shape[2]),
+        gain.reshape(1, -1),
+        freq,
+        lengths,
+        wq,
+        wk,
+        wv,
+        wo,
+        aq.T,
+        bq,
+        ak.T,
+        bk,
+        av.T,
+        bv,
+        ao.T,
+        bo,
+        keys.reshape(slots, head),
+        vals.reshape(slots, head),
+    )
+    return out.reshape(steps, pool, o_cols)
+
+
 def solution(mesh):
     in_specs = (
         P(None, ("groups", "pool"), None),
@@ -189,5 +698,9 @@
     )
     out_specs = P(None, "groups", "pool")
     return jax.shard_map(
-        on_device, mesh=mesh, in_specs=in_specs, out_specs=out_specs, check_vma=False
-    )
+        functools.partial(on_device_fused, mesh.shape["pool"], mesh.shape["tensor"]),
+        mesh=mesh,
+        in_specs=in_specs,
+        out_specs=out_specs,
+        check_vma=False,
+    )

time: 277 us -> 71.6 us (0.26)
  waiting for transfers between devices: 74.7 us -> 0 us
  Pallas kernels: 0 us -> 67.2 us
  blocking collectives: 54.6 us -> 0 us
  other arithmetic: 49.9 us -> 0.09 us
  local copies, waits for them, and re-layouts: 47.2 us -> 3.45 us
  matrix products: 28.2 us -> 0 us
  between operations: 14.3 us -> 0.67 us
  starting transfers between devices: 6.51 us -> 0 us
    pallas_call x0 -> x1, Pallas kernels: none -> 67.2 us  [on_device_fused(): pl.pallas_call(functools.partial(layer_kernel, pool, tensor, steps, kv_he...]
    unnamed x1 -> x0, other arithmetic: 46.5 us -> none
    all_gather x3 -> x0, blocking collectives: 41.9 us -> none  [the longest x1 14.4 us: on_device(): lax.all_gather(key_adapter_second, 'pool', axis=0, tiled=True)]
    all_gather x6 -> x0, waiting for transfers between devices: 37.4 us -> none  [the longest x1 29.2 us: on_device(): lax.all_gather(output_adapter_first, 'pool', axis=1, tiled=True)]
    unnamed x8 -> x0, waiting for transfers between devices: 37.3 us -> none
    unnamed x21 -> x0, local copies, waits for them, and re-layouts: 30.1 us -> none
    dot_general x9 -> x0, matrix products: 28.2 us -> none  [the longest x3 11.3 us: combine_adapter_weight(): jnp.dot(factor_a, factor_b, preferred_element_type=jnp.float32)]
    psum x1 -> x0, blocking collectives: 12.8 us -> none  [on_device(): result = lax.psum(partial_out, 'tensor').astype(jnp.bfloat16)]
  transfers between devices with their start and end apart: 8 -> 0, of which waited for: 3 -> 0; matrix products, arithmetic and copies ran while one was open for 39% -> 0% of each run, Pallas kernels for 0% -> 0%
where the time goes in v1:
time: 71.6 us; the launch traced here: 71.4 us
  Pallas kernels  67.2 us (94%)
  local copies, waits for them, and re-layouts  3.45 us (5%)
    pallas_call x1, Pallas kernels, on_device_fused(): pl.pallas_call(functools.partial(layer_kernel, pool, tensor, steps, kv_he...  67.2 us
    reshape x1, local copies, waits for them, and re-layouts, on_device_fused(): return out.reshape(steps, pool, o_cols)  1.5 us

profile of v1, /device:TPU:0, one launch (start us, length us, event | category | flops | bytes accessed | tf_op | source)
XLA Modules:
  0.0 71.4 jit_solution(17349503477158364812)
XLA Ops:
  0.7 0.1 pad_maximum_fusion
  0.7 0.6 broadcast_in_dim.2.freq_ref
  1.3 1.3 %reshape.17.gain_ref = bf16[1,8192]{1,0:T(2,128)(2,1)} reshape(bf16[8192]{0:T(1024)(128)(2,1)} %param.18) | data formatting | bytes 32768 | tf_op jit(solution)/shard_map/reshape | solution.py:658
  2.7 67.2 %shard_map.163 = bf16[16,2048]{1,0:T(8,128)(2,1)} custom-call(bf16[4,8192]{1,0:T(4,128)(2,1)} %bitcast.13, bf16[1,8192]{1,0:T(2,128)(2,1)} %reshape.17.gain_ref, f32[8,128]{1,0:T(8,128)} %broadcast_in_dim.2.freq_ref, s32[1]{0:T(128)S(6)} %copy.18.len_ref, bf16[2048,2048]{1,0:T(8,128)(2,1)} %wq_hbm.1, bf16[2048,256]{1,0:T(8,128)(2,1)} %wk_hbm.1, ...), custom_call_target="tpu_custom_call" | custom-call | tf_op jit(solution)/shard_map/pallas_call | solution.py:618
  69.9 1.5 %reshape.20 = bf16[4,4,2048]{2,1,0:T(4,128)(2,1)} reshape(bf16[16,2048]{1,0:T(8,128)(2,1)} %shard_map.163) | data formatting | bytes 131072 | tf_op jit(solution)/shard_map/reshape | solution.py:676
  (1 shorter events, 0.0 us)

commit v2 on v1

--- a/solution.py
+++ b/solution.py
@@ -3,6 +3,7 @@
 
 import jax
 import jax.numpy as jnp
+import numpy as np
 from jax import lax
 from jax.experimental import pallas as pl
 from jax.experimental.pallas import tpu as pltpu
@@ -255,25 +256,34 @@
         pltpu.make_async_copy(vals_hbm, vals, w_sem.at[5]),
     ]
 
-    def pieces(dst, src):
+    def pieces(dst, src, split):
         rows = at_block(src, rank)
+
+        def shared(ref, size):
+            if not split:
+                return ref.at[:, at_block(dst, size)]
+            return ref.at[:, at_block(dst * tensor + ten, size // tensor)]
+
+        def lands(ref, size):
+            return ref.at[rows, at_block(ten, size // tensor) if split else pl.ds(0, size)]
+
         return [
-            (aq_hbm.at[:, at_block(dst, depth)], a_in.at[0, rows, :]),
+            (shared(aq_hbm, depth), lands(a_in.at[0], depth)),
             (bq_hbm.at[:, at_block(ten, q_cols)], b_in.at[rows, pl.ds(0, q_cols)]),
-            (ak_hbm.at[:, at_block(dst, depth)], a_in.at[1, rows, :]),
+            (shared(ak_hbm, depth), lands(a_in.at[1], depth)),
             (bk_hbm.at[:, at_block(ten, kv_cols)], b_in.at[rows, pl.ds(q_cols, kv_cols)]),
-            (av_hbm.at[:, at_block(dst, depth)], a_in.at[2, rows, :]),
+            (shared(av_hbm, depth), lands(a_in.at[2], depth)),
             (
                 bv_hbm.at[:, at_block(ten, kv_cols)],
                 b_in.at[rows, pl.ds(q_cols + kv_cols, kv_cols)],
             ),
             (ao_hbm.at[:, at_block(ten, o_rows)], a_out.at[rows, :]),
-            (bo_hbm.at[:, at_block(dst, o_cols)], b_out.at[rows, :]),
+            (shared(bo_hbm, o_cols), lands(b_out, o_cols)),
         ]
 
     own = [
         pltpu.make_async_copy(src, dst, own_sem.at[i])
-        for i, (src, dst) in enumerate(pieces(me, me))
+        for i, (src, dst) in enumerate(pieces(me, me, False))
     ]
     for copy in own[:6] + loads[:3]:
         copy.start()
@@ -291,19 +301,6 @@
             device_id_type=MESH,
         )
 
-    fold = 16 // steps
-    states = x_ref[...].astype(f32)
-    mean = jnp.mean(states * states, -1, keepdims=True)
-    normed = states * lax.rsqrt(mean + norm_eps) * gain_ref[...].astype(f32)
-    width = depth // fold
-    for dst in range(pool):
-        folded = jnp.concatenate(
-            [normed[:, dst * depth + i * width : dst * depth + (i + 1) * width] for i in range(fold)],
-            0,
-        )
-        x_send[dst] = folded.astype(bf16)
-    pl.semaphore_wait(barrier, pool + tensor - 2)
-
     def to_pool(kind, off, src, dst_ref):
         return pltpu.make_async_remote_copy(
             src_ref=src,
@@ -316,18 +313,36 @@
 
     def sends(off):
         dst, _ = peer(off, "pool", pool)
-        out = [to_pool(i, off, a, b) for i, (a, b) in enumerate(pieces(dst, me))]
+        out = [to_pool(i, off, a, b) for i, (a, b) in enumerate(pieces(dst, me, True))]
         return out + [to_pool(8, off, x_send.at[dst], x_recv.at[me])]
 
     def arrivals(off):
         _, src = peer(off, "pool", pool)
-        out = [to_pool(i, off, b, b) for i, (a, b) in enumerate(pieces(me, src))]
+        out = [to_pool(i, off, b, b) for i, (a, b) in enumerate(pieces(me, src, True))]
         return out + [to_pool(8, off, x_recv.at[src], x_recv.at[src])]
 
     offs = list(range(1, pool))
     sent = {off: sends(off) for off in offs}
     come = {off: arrivals(off) for off in offs}
-    for kind in (8, 0, 1, 2, 3, 4, 5, 6, 7):
+    pl.semaphore_wait(barrier, pool + tensor - 2)
+    for kind in (0, 2, 4):
+        for off in offs:
+            sent[off][kind].start()
+
+    fold = 16 // steps
+    gain = gain_ref[...].astype(f32)
+    gain = jnp.concatenate([gain[i : i + 1] for i in range(gain.shape[0])], 1)
+    states = x_ref[...].astype(f32)
+    mean = jnp.mean(states * states, -1, keepdims=True)
+    normed = states * lax.rsqrt(mean + norm_eps) * gain
+    width = depth // fold
+    for dst in range(pool):
+        folded = jnp.concatenate(
+            [normed[:, dst * depth + i * width : dst * depth + (i + 1) * width] for i in range(fold)],
+            0,
+        )
+        x_send[dst] = folded.astype(bf16)
+    for kind in (8, 1, 3, 5, 6, 7):
         for off in offs:
             sent[off][kind].start()
     for copy in own[6:] + loads[3:]:
@@ -337,8 +352,46 @@
         for kind in kinds:
             if kind < 8:
                 own[kind].wait()
-            for off in offs:
+            if kind not in (0, 2, 4, 7):
+                for off in offs:
+                    come[off][kind].wait_recv()
+
+    def to_tensor(kind, off, src, dst_ref):
+        return pltpu.make_async_remote_copy(
+            src_ref=src,
+            dst_ref=dst_ref,
+            send_sem=t_send_sem.at[kind, off],
+            recv_sem=t_recv_sem.at[kind, off],
+            device_id={"tensor": peer(off, "tensor", tensor)[0]},
+            device_id_type=MESH,
+        )
+
+    t_offs = list(range(1, tensor))
+    forwarded, forwards_come = [], [[], []]
+
+    def forward(slot, buffer, kinds):
+        for off in offs:
+            _, src = peer(off, "pool", pool)
+            for kind in kinds:
                 come[off][kind].wait_recv()
+            for t_off in t_offs:
+                _, t_src = peer(t_off, "tensor", tensor)
+                kind = 2 + slot * pool + off
+
+                def part_of(owner):
+                    columns = at_block(owner, buffer.shape[-1] // tensor)
+                    if len(buffer.shape) == 3:
+                        return buffer.at[:, at_block(src, rank), columns]
+                    return buffer.at[at_block(src, rank), columns]
+
+                copy = to_tensor(kind, t_off, part_of(ten), part_of(ten))
+                copy.start()
+                forwarded.append(copy)
+                forwards_come[slot].append(
+                    to_tensor(kind, t_off, part_of(t_src), part_of(t_src))
+                )
+
+    forward(0, a_in, (0, 2, 4))
 
     x_recv[me] = x_send[me]
     wait_kinds((8,))
@@ -375,6 +428,8 @@
 
         lax.fori_loop(0, count // tile, one, 0)
 
+    for copy in forwards_come[0]:
+        copy.wait_recv()
     wait_kinds((0, 1))
     loads[0].wait()
     project(0, 0, q_cols)
@@ -398,7 +453,10 @@
         rs_come.append(to_pool(9, off, rs_recv.at[src], rs_recv.at[src]))
     rs_recv[me] = rs_send[me]
 
+    forward(1, b_out, (7,))
     wait_kinds((6, 7))
+    for copy in forwards_come[1]:
+        copy.wait_recv()
     loads[3].wait()
     a_cols[...] = a_out[...].T
 
@@ -525,17 +583,6 @@
 
     share = o_cols // tensor
 
-    def to_tensor(kind, off, src, dst_ref):
-        return pltpu.make_async_remote_copy(
-            src_ref=src,
-            dst_ref=dst_ref,
-            send_sem=t_send_sem.at[kind, off],
-            recv_sem=t_recv_sem.at[kind, off],
-            device_id={"tensor": peer(off, "tensor", tensor)[0]},
-            device_id_type=MESH,
-        )
-
-    t_offs = list(range(1, tensor))
     o_sent, o_come = [], []
     for off in t_offs:
         dst, src = peer(off, "tensor", tensor)
@@ -563,11 +610,15 @@
     for copy in f_come:
         copy.wait_recv()
     for src in range(tensor):
-        out_ref[:, src * share : (src + 1) * share] = fin[src]
+        block = fin[src].astype(f32)
+        for s in range(steps):
+            out_ref[s, :, src * share : (src + 1) * share] = block[
+                s * pool : (s + 1) * pool
+            ].astype(bf16)
     for off in offs:
         for copy in sent[off]:
             copy.wait_send()
-    for copy in rs_sent + h_sent + o_sent + f_sent:
+    for copy in forwarded + rs_sent + h_sent + o_sent + f_sent:
         copy.wait_send()
 
 
@@ -590,6 +641,8 @@
         and wo.shape[0] == wq.shape[0]
         and wo.shape[1] % (128 * tensor) == 0
         and wo.shape[1] % 256 == 0
+        and wq.shape[0] % (128 * tensor) == 0
+        and hidden.shape[2] % 128 == 0
         and (keys.shape[1] * keys.shape[2]) % 1024 == 0
         and wq.shape[0] * (wq.shape[1] + 2 * wk.shape[1] + wo.shape[1]) <= 12 * 1024 * 1024
     )
@@ -609,15 +662,14 @@
     q_rows = q_cols // head * steps
     slots = keys.shape[1] * kv_heads
     tokens = pool * steps
-    half = jnp.arange(head // 2, dtype=f32)
-    frequency = rope_base ** (-(half * 2.0 / head))
-    freq = jnp.broadcast_to(jnp.concatenate([frequency, frequency])[None, :], (8, head))
+    frequency = rope_base ** (-(np.arange(head // 2) * 2.0 / head))
+    freq = np.broadcast_to(np.tile(frequency, 2)[None, :], (8, head)).astype(np.float32)
     vmem = pl.BlockSpec(memory_space=pltpu.VMEM)
     hbm = pl.BlockSpec(memory_space=pl.ANY)
     share = o_cols // tensor
     out = pl.pallas_call(
         functools.partial(layer_kernel, pool, tensor, steps, kv_heads),
-        out_shape=jax.ShapeDtypeStruct((tokens, o_cols), bf16),
+        out_shape=jax.ShapeDtypeStruct((steps, pool, o_cols), bf16),
         in_specs=[vmem, vmem, vmem, pl.BlockSpec(memory_space=pltpu.SMEM)] + [hbm] * 14,
         out_specs=vmem,
         scratch_shapes=[
@@ -647,16 +699,16 @@
             pltpu.SemaphoreType.DMA((8,)),
             pltpu.SemaphoreType.DMA((11, pool)),
             pltpu.SemaphoreType.DMA((11, pool)),
-            pltpu.SemaphoreType.DMA((2, tensor)),
-            pltpu.SemaphoreType.DMA((2, tensor)),
+            pltpu.SemaphoreType.DMA((2 + 2 * pool, tensor)),
+            pltpu.SemaphoreType.DMA((2 + 2 * pool, tensor)),
         ],
         compiler_params=pltpu.CompilerParams(
             collective_id=0, has_side_effects=True, vmem_limit_bytes=56 * 1024 * 1024
         ),
     )(
         hidden.reshape(steps, hidden.shape[2]),
-        gain.reshape(1, -1),
-        freq,
+        gain.reshape(-1, 128),
+        jnp.asarray(freq),
         lengths,
         wq,
         wk,
@@ -673,7 +725,7 @@
         keys.reshape(slots, head),
         vals.reshape(slots, head),
     )
-    return out.reshape(steps, pool, o_cols)
+    return out
 
 
 def solution(mesh):

time: 71.6 us -> 58.9 us (0.82)
  Pallas kernels: 67.2 us -> 56.5 us
  local copies, waits for them, and re-layouts: 3.45 us -> 1.49 us
    pallas_call x1, Pallas kernels: 67.2 us -> 56.5 us  [on_device_fused(): pl.pallas_call(functools.partial(layer_kernel, pool, tensor, steps, kv_he...]
    reshape x2 -> x0, local copies, waits for them, and re-layouts: 2.85 us -> none  [the longest x1 1.5 us: on_device_fused(): return out.reshape(steps, pool, o_cols)]
    unnamed x0 -> x1, local copies, waits for them, and re-layouts: none -> 1.49 us
where the time goes in v2:
time: 58.9 us; the launch traced here: 58.7 us
  Pallas kernels  56.5 us (96%)
  local copies, waits for them, and re-layouts  1.49 us (3%)
  between operations  0.66 us (1%)
    pallas_call x1, Pallas kernels, on_device_fused(): pl.pallas_call(functools.partial(layer_kernel, pool, tensor, steps, kv_he...  56.5 us
    unnamed x1, local copies, waits for them, and re-layouts  1.49 us

profile of v2, /device:TPU:0, one launch (start us, length us, event | category | flops | bytes accessed | tf_op | source)
XLA Modules:
  0.0 58.7 jit_solution(12765362717413342559)
XLA Ops:
  0.7 56.5 %shard_map.172 = bf16[4,4,2048]{2,1,0:T(4,128)(2,1)} custom-call(bf16[4,8192]{1,0:T(4,128)(2,1)} %bitcast.14, bf16[64,128]{1,0:T(8,128)(2,1)} %bitcast.15, f32[8,128]{1,0:T(8,128)} %constant.2.clone.freq_ref, s32[1]{0:T(128)S(6)} %copy.20.len_ref, bf16[2048,2048]{1,0:T(8,128)(2,1)} %wq_hbm.1, bf16[2048,256]{1,0:T(8,128)(2,1)} %wk_hbm.1, ...), custom_call_target="tpu_custom_call" | custom-call | tf_op jit(solution)/shard_map/pallas_call | solution.py:670
  57.2 1.5 %copy.21 = bf16[4,4,2048]{2,1,0:T(4,128)(2,1)} copy(bf16[4,4,2048]{2,1,0:T(4,128)(2,1)} %shard_map.172) | data formatting | bytes 131072

commit v3 on v2

--- a/solution.py
+++ b/solution.py
@@ -179,6 +179,7 @@
     tensor,
     steps,
     kv_heads,
+    q_parts,
     x_ref,
     gain_ref,
     freq_ref,
@@ -207,6 +208,7 @@
     a_out,
     b_out,
     a_cols,
+    turn,
     x_send,
     x_recv,
     x_full,
@@ -267,12 +269,12 @@
         def lands(ref, size):
             return ref.at[rows, at_block(ten, size // tensor) if split else pl.ds(0, size)]
 
-        return [
+        part = q_cols // q_parts
+        listed = [
             (shared(aq_hbm, depth), lands(a_in.at[0], depth)),
-            (bq_hbm.at[:, at_block(ten, q_cols)], b_in.at[rows, pl.ds(0, q_cols)]),
             (shared(ak_hbm, depth), lands(a_in.at[1], depth)),
+            (shared(av_hbm, depth), lands(a_in.at[2], depth)),
             (bk_hbm.at[:, at_block(ten, kv_cols)], b_in.at[rows, pl.ds(q_cols, kv_cols)]),
-            (shared(av_hbm, depth), lands(a_in.at[2], depth)),
             (
                 bv_hbm.at[:, at_block(ten, kv_cols)],
                 b_in.at[rows, pl.ds(q_cols + kv_cols, kv_cols)],
@@ -280,12 +282,22 @@
             (ao_hbm.at[:, at_block(ten, o_rows)], a_out.at[rows, :]),
             (shared(bo_hbm, o_cols), lands(b_out, o_cols)),
         ]
+        for i in range(q_parts):
+            listed.append(
+                (
+                    bq_hbm.at[:, at_block(ten * q_parts + i, part)],
+                    b_in.at[rows, pl.ds(i * part, part)],
+                )
+            )
+        return listed
 
     own = [
         pltpu.make_async_copy(src, dst, own_sem.at[i])
         for i, (src, dst) in enumerate(pieces(me, me, False))
     ]
-    for copy in own[:6] + loads[:3]:
+    shares_a, shares_b = (0, 1, 2), 6
+    x_kind = 7 + q_parts
+    for copy in loads[:3] + own:
         copy.start()
 
     barrier = pltpu.get_barrier_semaphore()
@@ -314,18 +326,18 @@
     def sends(off):
         dst, _ = peer(off, "pool", pool)
         out = [to_pool(i, off, a, b) for i, (a, b) in enumerate(pieces(dst, me, True))]
-        return out + [to_pool(8, off, x_send.at[dst], x_recv.at[me])]
+        return out + [to_pool(x_kind, off, x_send.at[dst], x_recv.at[me])]
 
     def arrivals(off):
         _, src = peer(off, "pool", pool)
         out = [to_pool(i, off, b, b) for i, (a, b) in enumerate(pieces(me, src, True))]
-        return out + [to_pool(8, off, x_recv.at[src], x_recv.at[src])]
+        return out + [to_pool(x_kind, off, x_recv.at[src], x_recv.at[src])]
 
     offs = list(range(1, pool))
     sent = {off: sends(off) for off in offs}
     come = {off: arrivals(off) for off in offs}
     pl.semaphore_wait(barrier, pool + tensor - 2)
-    for kind in (0, 2, 4):
+    for kind in shares_a:
         for off in offs:
             sent[off][kind].start()
 
@@ -342,17 +354,17 @@
             0,
         )
         x_send[dst] = folded.astype(bf16)
-    for kind in (8, 1, 3, 5, 6, 7):
+    for kind in (x_kind, 3, 4) + tuple(range(7, 7 + q_parts)):
         for off in offs:
             sent[off][kind].start()
-    for copy in own[6:] + loads[3:]:
+    for copy in loads[3:]:
         copy.start()
 
     def wait_kinds(kinds):
         for kind in kinds:
-            if kind < 8:
+            if kind < x_kind:
                 own[kind].wait()
-            if kind not in (0, 2, 4, 7):
+            if kind not in (0, 1, 2, 6):
                 for off in offs:
                     come[off][kind].wait_recv()
 
@@ -391,10 +403,19 @@
                     to_tensor(kind, t_off, part_of(t_src), part_of(t_src))
                 )
 
-    forward(0, a_in, (0, 2, 4))
+    forward(0, a_in, shares_a)
+
+    length = len_ref[0]
+    lanes = freq_ref.shape[1]
+    spare = freq_ref.shape[0]
+    step_of = lax.rem(lax.broadcasted_iota(jnp.int32, (spare, lanes), 0), steps)
+    angles = (length + step_of).astype(f32) * freq_ref[...]
+    lane = lax.broadcasted_iota(jnp.int32, (spare, lanes), 1)
+    turn[0] = jnp.cos(angles)
+    turn[1] = jnp.where(lane < head // 2, -jnp.sin(angles), jnp.sin(angles))
 
     x_recv[me] = x_send[me]
-    wait_kinds((8,))
+    wait_kinds((x_kind,))
     rows = []
     for src in range(pool):
         got = x_recv[src].astype(f32)
@@ -413,13 +434,11 @@
         return (w_ref[pl.ds(row0, chunk), column].astype(f32) + low_rank).astype(bf16)
 
     def project(which, first, count):
-        a_cols[...] = a_in[which].T
-
         def one(j, carry):
             column = pl.ds(pl.multiple_of(first + j * tile, tile), tile)
             total = jnp.zeros((tokens, tile), f32)
             for row0 in range(0, depth, chunk):
-                block = merged(a_cols, row0, b_in, w_in, column)
+                block = merged(a_cols.at[which], row0, b_in, w_in, column)
                 total += jnp.dot(
                     x_full[:, row0 : row0 + chunk], block, preferred_element_type=f32
                 )
@@ -430,15 +449,17 @@
 
     for copy in forwards_come[0]:
         copy.wait_recv()
-    wait_kinds((0, 1))
-    loads[0].wait()
-    project(0, 0, q_cols)
-    wait_kinds((2, 3))
-    loads[1].wait()
+    wait_kinds(shares_a)
+    for which in range(3):
+        a_cols[which] = a_in[which].T
+    wait_kinds((3, 4))
+    for load in loads[:3]:
+        load.wait()
     project(1, q_cols, kv_cols)
-    wait_kinds((4, 5))
-    loads[2].wait()
     project(2, q_cols + kv_cols, kv_cols)
+    for i in range(q_parts):
+        wait_kinds((7 + i,))
+        project(0, i * (q_cols // q_parts), q_cols // q_parts)
 
     half = in_cols // 2
     for dst in range(pool):
@@ -447,26 +468,15 @@
     rs_sent, rs_come = [], []
     for off in offs:
         dst, src = peer(off, "pool", pool)
-        copy = to_pool(9, off, rs_send.at[dst], rs_recv.at[me])
+        copy = to_pool(x_kind + 1, off, rs_send.at[dst], rs_recv.at[me])
         copy.start()
         rs_sent.append(copy)
-        rs_come.append(to_pool(9, off, rs_recv.at[src], rs_recv.at[src]))
+        rs_come.append(to_pool(x_kind + 1, off, rs_recv.at[src], rs_recv.at[src]))
     rs_recv[me] = rs_send[me]
 
-    forward(1, b_out, (7,))
-    wait_kinds((6, 7))
-    for copy in forwards_come[1]:
-        copy.wait_recv()
-    loads[3].wait()
-    a_cols[...] = a_out[...].T
-
-    def merge_out(j, carry):
-        column = pl.ds(pl.multiple_of(j * tile, tile), tile)
-        for row0 in range(0, o_rows, chunk):
-            w_out[pl.ds(row0, chunk), column] = merged(a_cols, row0, b_out, w_out, column)
-        return carry
-
-    lax.fori_loop(0, o_cols // tile, merge_out, 0)
+    for kind in (5, 6):
+        for off in offs:
+            sent[off][kind].start()
 
     for copy in rs_come:
         copy.wait_recv()
@@ -475,15 +485,6 @@
         summed = summed + rs_recv[src]
     flat = jnp.concatenate([summed[:steps], summed[steps:]], 1)
 
-    length = len_ref[0]
-    lanes = freq_ref.shape[1]
-    spare = freq_ref.shape[0]
-    step_of = lax.rem(lax.broadcasted_iota(jnp.int32, (spare, lanes), 0), steps)
-    angles = (length + step_of).astype(f32) * freq_ref[...]
-    cosine = jnp.cos(angles)
-    lane = lax.broadcasted_iota(jnp.int32, (spare, lanes), 1)
-    sine = jnp.where(lane < head // 2, -jnp.sin(angles), jnp.sin(angles))
-
     def stack(first, count):
         return jnp.concatenate(
             [flat[:, first + h * head : first + (h + 1) * head] for h in range(count)], 0
@@ -491,8 +492,8 @@
 
     def turned(values):
         turns = values.shape[0] // spare
-        cos_all = jnp.concatenate([cosine] * turns, 0)
-        sin_all = jnp.concatenate([sine] * turns, 0)
+        cos_all = jnp.concatenate([turn[0]] * turns, 0)
+        sin_all = jnp.concatenate([turn[1]] * turns, 0)
         return (values * cos_all + pltpu.roll(values, head // 2, 1) * sin_all).astype(bf16)
 
     queries = turned(stack(0, q_heads))
@@ -561,11 +562,26 @@
     h_sent, h_come = [], []
     for off in offs:
         _, src = peer(off, "pool", pool)
-        copy = to_pool(10, off, h_send, h_recv.at[me])
+        copy = to_pool(x_kind + 2, off, h_send, h_recv.at[me])
         copy.start()
         h_sent.append(copy)
-        h_come.append(to_pool(10, off, h_recv.at[src], h_recv.at[src]))
+        h_come.append(to_pool(x_kind + 2, off, h_recv.at[src], h_recv.at[src]))
     h_recv[me] = h_send[...]
+    forward(1, b_out, (6,))
+    wait_kinds((5, 6))
+    for copy in forwards_come[1]:
+        copy.wait_recv()
+    loads[3].wait()
+    a_cols[0] = a_out[...].T
+
+    def merge_out(j, carry):
+        column = pl.ds(pl.multiple_of(j * tile, tile), tile)
+        for row0 in range(0, o_rows, chunk):
+            w_out[pl.ds(row0, chunk), column] = merged(a_cols.at[0], row0, b_out, w_out, column)
+        return carry
+
+    lax.fori_loop(0, o_cols // tile, merge_out, 0)
+
     for copy in h_come:
         copy.wait_recv()
     every = [h_recv[src].astype(f32) for src in range(pool)]
@@ -667,8 +683,9 @@
     vmem = pl.BlockSpec(memory_space=pltpu.VMEM)
     hbm = pl.BlockSpec(memory_space=pl.ANY)
     share = o_cols // tensor
+    q_parts = math.gcd(q_cols // 256, 4)
     out = pl.pallas_call(
-        functools.partial(layer_kernel, pool, tensor, steps, kv_heads),
+        functools.partial(layer_kernel, pool, tensor, steps, kv_heads, q_parts),
         out_shape=jax.ShapeDtypeStruct((steps, pool, o_cols), bf16),
         in_specs=[vmem, vmem, vmem, pl.BlockSpec(memory_space=pltpu.SMEM)] + [hbm] * 14,
         out_specs=vmem,
@@ -681,7 +698,8 @@
             pltpu.VMEM((pool * rank, in_cols), bf16),
             pltpu.VMEM((pool * rank, o_rows), bf16),
             pltpu.VMEM((pool * rank, o_cols), bf16),
-            pltpu.VMEM((depth, pool * rank), bf16),
+            pltpu.VMEM((3, depth, pool * rank), bf16),
+            pltpu.VMEM((2, 8, head), f32),
             pltpu.VMEM((pool, 16, depth * steps // 16), bf16),
             pltpu.VMEM((pool, 16, depth * steps // 16), bf16),
             pltpu.VMEM((tokens, depth), bf16),
@@ -696,9 +714,9 @@
             pltpu.VMEM((tensor, tokens, share), f32),
             pltpu.VMEM((tensor, tokens, share), bf16),
             pltpu.SemaphoreType.DMA((6,)),
-            pltpu.SemaphoreType.DMA((8,)),
-            pltpu.SemaphoreType.DMA((11, pool)),
-            pltpu.SemaphoreType.DMA((11, pool)),
+            pltpu.SemaphoreType.DMA((7 + q_parts,)),
+            pltpu.SemaphoreType.DMA((10 + q_parts, pool)),
+            pltpu.SemaphoreType.DMA((10 + q_parts, pool)),
             pltpu.SemaphoreType.DMA((2 + 2 * pool, tensor)),
             pltpu.SemaphoreType.DMA((2 + 2 * pool, tensor)),
         ],

time: 58.9 us -> 59.1 us (level)
  no operation moved by 1% of the time
where the time goes in v3:
time: 59.1 us; the launch traced here: 58.9 us
  Pallas kernels  56.8 us (96%)
  local copies, waits for them, and re-layouts  1.49 us (3%)
  between operations  0.66 us (1%)
    pallas_call x1, Pallas kernels, on_device_fused(): pl.pallas_call(functools.partial(layer_kernel, pool, tensor, steps, kv_he...  56.8 us
    unnamed x1, local copies, waits for them, and re-layouts  1.49 us

profile of v3, /device:TPU:0, one launch (start us, length us, event | category | flops | bytes accessed | tf_op | source)
XLA Modules:
  0.0 58.9 jit_solution(12067196937679373266)
XLA Ops:
  0.7 56.8 %shard_map.172 = bf16[4,4,2048]{2,1,0:T(4,128)(2,1)} custom-call(bf16[4,8192]{1,0:T(4,128)(2,1)} %bitcast.14, bf16[64,128]{1,0:T(8,128)(2,1)} %bitcast.15, f32[8,128]{1,0:T(8,128)} %constant.2.clone.freq_ref, s32[1]{0:T(128)S(6)} %copy.20.len_ref, bf16[2048,2048]{1,0:T(8,128)(2,1)} %wq_hbm.1, bf16[2048,256]{1,0:T(8,128)(2,1)} %wk_hbm.1, ...), custom_call_target="tpu_custom_call" | custom-call | tf_op jit(solution)/shard_map/pallas_call | solution.py:687
  57.4 1.5 %copy.21 = bf16[4,4,2048]{2,1,0:T(4,128)(2,1)} copy(bf16[4,4,2048]{2,1,0:T(4,128)(2,1)} %shard_map.172) | data formatting | bytes 131072

commit v4 on v3

--- a/solution.py
+++ b/solution.py
@@ -297,7 +297,7 @@
     ]
     shares_a, shares_b = (0, 1, 2), 6
     x_kind = 7 + q_parts
-    for copy in loads[:3] + own:
+    for copy in own[:5] + own[7:]:
         copy.start()
 
     barrier = pltpu.get_barrier_semaphore()
@@ -357,7 +357,7 @@
     for kind in (x_kind, 3, 4) + tuple(range(7, 7 + q_parts)):
         for off in offs:
             sent[off][kind].start()
-    for copy in loads[3:]:
+    for copy in loads[:3]:
         copy.start()
 
     def wait_kinds(kinds):
@@ -404,6 +404,12 @@
                 )
 
     forward(0, a_in, shares_a)
+    for copy in loads[3:] + own[5:7]:
+        copy.start()
+    for kind in (5, 6):
+        for off in offs:
+            sent[off][kind].start()
+
 
     length = len_ref[0]
     lanes = freq_ref.shape[1]
@@ -473,10 +479,6 @@
         rs_sent.append(copy)
         rs_come.append(to_pool(x_kind + 1, off, rs_recv.at[src], rs_recv.at[src]))
     rs_recv[me] = rs_send[me]
-
-    for kind in (5, 6):
-        for off in offs:
-            sent[off][kind].start()
 
     for copy in rs_come:
         copy.wait_recv()

time: 59.1 us -> 55.9 us (0.946)
  Pallas kernels: 56.8 us -> 53.6 us
    pallas_call x1, Pallas kernels: 56.8 us -> 53.6 us  [on_device_fused(): pl.pallas_call(functools.partial(layer_kernel, pool, tensor, steps, kv_he...]
where the time goes in v4:
time: 55.9 us; the launch traced here: 55.7 us
  Pallas kernels  53.6 us (96%)
  local copies, waits for them, and re-layouts  1.49 us (3%)
  between operations  0.66 us (1%)
    pallas_call x1, Pallas kernels, on_device_fused(): pl.pallas_call(functools.partial(layer_kernel, pool, tensor, steps, kv_he...  53.6 us
    unnamed x1, local copies, waits for them, and re-layouts  1.49 us

profile of v4, /device:TPU:0, one launch (start us, length us, event | category | flops | bytes accessed | tf_op | source)
XLA Modules:
  0.0 55.7 jit_solution(16073122634317016517)
XLA Ops:
  0.7 53.6 %shard_map.172 = bf16[4,4,2048]{2,1,0:T(4,128)(2,1)} custom-call(bf16[4,8192]{1,0:T(4,128)(2,1)} %bitcast.14, bf16[64,128]{1,0:T(8,128)(2,1)} %bitcast.15, f32[8,128]{1,0:T(8,128)} %constant.2.clone.freq_ref, s32[1]{0:T(128)S(6)} %copy.20.len_ref, bf16[2048,2048]{1,0:T(8,128)(2,1)} %wq_hbm.1, bf16[2048,256]{1,0:T(8,128)(2,1)} %wk_hbm.1, ...), custom_call_target="tpu_custom_call" | custom-call | tf_op jit(solution)/shard_map/pallas_call | solution.py:689
  54.2 1.5 %copy.21 = bf16[4,4,2048]{2,1,0:T(4,128)(2,1)} copy(bf16[4,4,2048]{2,1,0:T(4,128)(2,1)} %shard_map.172) | data formatting | bytes 131072
